TPU v7x, 32 devices: a whole 2x2x4 slice. The times are simulated.
32 devices in a mesh: virt: 8 (over y, x, core), opair: 4 (over z).
Axes of the slice: x: 2, y: 2, z: 4, core: 2. Of those that a mesh axis runs over, the one named last changes fastest.
Arguments:
- amplitudes: bfloat16 [64, 6144], P('virt', 'opair'), may hold values from -6 to 6
- integrals: bfloat16 [6144, 1024, 128], P('opair', 'virt'), may hold values from -0.078125 to 0.078125
- driver: bfloat16 [64, 1024, 128], P('opair', 'virt'), may hold values from -6 to 6
- eps_occ: float32 [200], replicated, may hold values from -2 to -0.5
- eps_vir: float32 [1024], replicated, may hold values from 0.2 to 2
- pair_occ: int32 [64, 2], P('opair'), may hold values from 0 to 199
- offsets: int32 [1024], P('virt'), may hold values from 0 to 896, as said below
- sizes: int32 [1024], P('virt'), may hold values from 64 to 128, as said below
Outputs:
- update: bfloat16 [64, 1024, 128], P('opair', 'virt')
Inputs may be any that keep to these rules, and one draw needn't show every extreme that they name: There are 8 irrep blocks, block k starting at k * 128; a's block starts at offsets[a], and every block is paired with some a. sizes[a] is the length of a's block; 128 is reached by some block in every draw.
All inputs are finite; a program needn't handle non-finite values.
Results may differ from a plain program's by a relative error of at most 0.001.
Values may be sent and summed in bfloat16 or wider, within the bound.
A program may use at most 128 MiB of HBM per device.

v0:
```python
import jax
import jax.numpy as jnp
from jax import lax
from jax.sharding import PartitionSpec as P


def local(amplitudes, integrals, driver, eps_occ, eps_vir, pair_occ, offsets, sizes):
    slab_rows, a_count, bwidth = integrals.shape
    own_rows = driver.shape[0]
    flat = integrals.reshape(slab_rows, a_count * bwidth)
    panel = lax.all_gather(amplitudes, "virt", axis=0, tiled=True)
    ladder = lax.psum_scatter(
        jnp.dot(panel, flat, preferred_element_type=jnp.float32),
        "opair",
        scatter_dimension=0,
        tiled=True,
    )
    ladder = ladder.reshape(own_rows, a_count, bwidth)
    pair_energy = jnp.take(eps_occ, pair_occ[:, 0]) + jnp.take(eps_occ, pair_occ[:, 1])
    column = jnp.arange(bwidth, dtype=jnp.int32)
    b_index = offsets[:, None] + jnp.minimum(column[None, :], sizes[:, None] - 1)
    e_pair = jnp.take(eps_vir, b_index)
    first = lax.axis_index("virt") * a_count
    e_first = lax.dynamic_slice_in_dim(eps_vir, first, a_count, 0)
    denominator = pair_energy[:, None, None] - e_first[None, :, None] - e_pair[None, :, :]
    value = (ladder + driver.astype(jnp.float32)) / denominator
    inside = column[None, None, :] < sizes[None, :, None]
    return jnp.where(inside, value, jnp.zeros_like(value)).astype(jnp.bfloat16)


def solution(mesh):
    placed = (
        P("virt", "opair"),
        P("opair", "virt", None),
        P("opair", "virt", None),
        P(),
        P(),
        P("opair", None),
        P("virt"),
        P("virt"),
    )
    return jax.shard_map(
        local, mesh=mesh, in_specs=placed, out_specs=P("opair", "virt", None), check_vma=False
    )
```

profile of v0, /device:TPU:0, one launch (start us, length us, event | category | flops | bytes accessed | tf_op | source)
XLA Modules:
  0.0 153.7 jit_solution(2406821569674145707)
XLA Ops:
  6.5 0.0 copy-start
  6.5 0.0 copy-start.5
  6.5 0.0 copy-start.4
  6.5 0.0 copy-start.1
  6.5 0.0 reduce-scatter.2.cloned.1.call-start
  6.6 10.9 %all_gather.3 = bf16[64,1536]{1,0:T(8,128)(2,1)S(1)} all-gather(bf16[8,1536]{1,0:T(8,128)(2,1)} %param.10), channel_id=1, replica_groups=mesh['virt'=8,'opair'=4] {'virt'}, dimensions={0}, use_global_device_ids=true | all-gather | bytes 221184 | tf_op jit(solution)/shard_map/all_gather | solution.py:11
  17.5 49.6 %fusion = f32[64,16384]{1,0:T(8,128)} fusion(bf16[64,1536]{1,0:T(8,128)(2,1)S(1)} %all_gather.3, bf16[192,8,128,128]{3,2,1,0:T(8,128)(2,1)} %bitcast.29), kind=kOutput, calls=%fused_computation.3 | convolution fusion | flops 3221225472 | bytes 54722560 | tf_op jit(solution)/shard_map/dot_general | solution.py:13
  67.1 0.0 copy-start.3
  67.1 0.0 copy-start.2
  67.1 0.0 reduce-scatter.2.cloned.1.call-update
  67.1 0.0 copy-done.5
  67.1 0.0 copy-done.4
  67.1 0.1 fusion.7
  67.2 0.0 copy-done.1
  67.3 65.3 %gather_fusion = f32[16384]{0:T(1024)S(1)} fusion(f32[1024]{0:T(1024)S(1)} %copy-done.1, s32[16384]{0:T(1024)S(1)} %fusion.7), kind=kCustom, calls=%fused_computation.2 | custom fusion | bytes 196608 | tf_op jit(solution)/shard_map/jit(_take)/gather | solution.py:22
  132.5 0.1 dynamic_slice.3
  132.6 0.0 copy-done.3
  132.6 0.0 copy-done
  132.6 0.7 gather_fusion.1
  133.3 0.7 gather_fusion.2
  134.0 0.1 broadcast_subtract_fusion
  134.1 0.1 iota_compare_fusion
  134.2 0.1 bitcast_select_fusion
  134.3 10.0 %reduce-scatter.2.cloned.1.call-done = f32[16,16384]{1,0:T(8,128)} async-done(((f32[64,16384]{1,0:T(8,128)}), f32[16,16384]{1,0:T(8,128)}) %reduce-scatter.2.cloned.1.call-update) | async-done | bytes 1048592 | tf_op jit(solution)/shard_map/reduce_scatter | solution.py:12
  144.3 1.4 copy.10
  145.7 0.0 copy-done.2
  145.7 1.2 fusion.5
  (4 shorter events, 0.0 us)
Async XLA Ops:
  6.5 126.1 %copy-start = (f32[200]{0:T(256)S(1)}, f32[200]{0:T(256)}, u32[]{:S(2)}) copy-start(f32[200]{0:T(256)} %param.13) | copy-start | bytes 2404
  6.5 60.6 %copy-start.5 = (s32[128]{0:T(128)S(1)}, s32[128]{0:T(128)}, u32[]{:S(2)}) copy-start(s32[128]{0:T(128)} %param.17) | copy-start | bytes 1540
  6.5 60.6 %copy-start.4 = (s32[128]{0:T(128)S(1)}, s32[128]{0:T(128)}, u32[]{:S(2)}) copy-start(s32[128]{0:T(128)} %param.16) | copy-start | bytes 1540
  6.5 60.7 %copy-start.1 = (f32[1024]{0:T(1024)S(1)}, f32[1024]{0:T(1024)}, u32[]{:S(2)}) copy-start(f32[1024]{0:T(1024)} %param.14) | copy-start | bytes 12292
  6.5 137.8 %reduce-scatter.2.cloned.1.call-start = ((), (), s32[]{:S(2)}) async-start(), calls=%async_computation.1 | async-start | bytes 5242880 | tf_op jit(solution)/shard_map/reduce_scatter | solution.py:12
  67.1 65.5 %copy-start.3 = (s32[16,2]{0,1:T(2,128)S(1)}, s32[16,2]{0,1:T(2,128)}, u32[]{:S(2)}) copy-start(s32[16,2]{0,1:T(2,128)} %param.15) | copy-start | bytes 388
  67.1 78.7 %copy-start.2 = (bf16[16,128,128]{2,1,0:T(8,128)(2,1)S(1)}, bf16[16,128,128]{2,1,0:T(8,128)(2,1)}, u32[]{:S(2)}) copy-start(bf16[16,128,128]{2,1,0:T(8,128)(2,1)} %param.12) | copy-start | bytes 1572868
Sparse Core Ops, SparseCore 0:
  67.2 77.0 reduce-scatter.1
where the time goes:
time: 154 us
  local copies, waits for them, and re-layouts  68.1 us (44%)
  matrix products  49.6 us (32%)
  between operations  13.5 us (9%)
  blocking collectives  10.9 us (7%)
  waiting for transfers between devices  10.1 us (7%)
  other arithmetic  1.55 us (1%)
    gather x1, local copies, waits for them, and re-layouts, local(): e_pair = jnp.take(eps_vir, b_index)  65.3 us
    dot_general x1, matrix products, local(): jnp.dot(panel, flat, preferred_element_type=jnp.float32)  49.6 us
    all_gather x1, blocking collectives, local(): panel = lax.all_gather(amplitudes, 'virt', axis=0, tiled=True)  10.9 us
    reduce_scatter x1, waiting for transfers between devices, local(): lax.psum_scatter(jnp.dot(panel, flat, preferred_element_type=jnp.float32)...  10 us
  transfers between devices with their start and end apart: 1, of which 1 were waited for; matrix products, arithmetic and copies ran while one was open for 44% of the time, Pallas kernels for 0%

commit v1 on v0

v1 whole, which is shorter than its diff:
```python
import functools

import jax
import jax.numpy as jnp
from jax import lax
from jax.experimental import pallas as pl
from jax.experimental.pallas import tpu as pltpu
from jax.sharding import PartitionSpec as P

MESH = pl.DeviceIdType.MESH
LANES = 128
LEVELS = 32000.0


def encode(x, out_ref, width):
    top = jnp.maximum(jnp.max(jnp.abs(x), axis=1, keepdims=True), 1e-30)
    code = jnp.broadcast_to(jnp.ceil(jnp.log2(top) * 64.0), (x.shape[0], LANES))
    gain = (jnp.exp2(code * (-1.0 / 64.0)) * LEVELS)[:, :1]
    out_ref[:, :width] = jnp.round(x * gain).astype(jnp.int32).astype(jnp.int16)
    out_ref[:, width:] = code.astype(jnp.int32).astype(jnp.int16)


def decode(in_ref, width):
    code = in_ref[:, width:].astype(jnp.int32).astype(jnp.float32)
    gain = (jnp.exp2(code * (1.0 / 64.0)) * (1.0 / LEVELS))[:, :1]
    return in_ref[:, :width].astype(jnp.int32).astype(jnp.float32) * gain


def kernel(
    n, nv, step_rows, slots,
    amp_ref, int_ref, driver_ref, pe_ref, ef_ref, ep_ref, in_ref, out_ref,
    panel32, panel, ibuf, acc, sbuf, rbuf,
    isem, asend, arecv, ssem, rsem,
):
    z = lax.axis_index("opair")
    v = lax.axis_index("virt")
    chunks, pairs, width = acc.shape
    rows = pairs // n
    slab, ca = ibuf.shape[1], ibuf.shape[2]
    last = n - 1

    def load(c):
        slot = lax.rem(c, slots)
        return pltpu.make_async_copy(
            int_ref.at[:, pl.ds(pl.multiple_of(c * ca, ca), ca), :], ibuf.at[slot], isem.at[slot]
        )

    for c in range(min(slots, chunks)):
        load(c).start()

    barrier = pltpu.get_barrier_semaphore()

    def greet(d, carry):
        peer = lax.rem(v + d, nv)
        pl.semaphore_signal(barrier, inc=1, device_id={"virt": peer}, device_id_type=MESH)
        return carry

    lax.fori_loop(1, nv, greet, 0)

    @pl.when(z > 0)
    def _():
        pl.semaphore_signal(barrier, inc=1, device_id={"opair": z - 1}, device_id_type=MESH)

    @pl.when(z < last)
    def _():
        pl.semaphore_signal(barrier, inc=1, device_id={"opair": z + 1}, device_id_type=MESH)

    panel32[v] = amp_ref[...].astype(jnp.float32)
    beside = jnp.where(z > 0, 1, 0) + jnp.where(z < last, 1, 0)
    pl.semaphore_wait(barrier, nv - 1 + beside)

    def share(d, slot):
        peer = lax.rem(v + d, nv)
        return pltpu.make_async_remote_copy(
            src_ref=panel32.at[slot],
            dst_ref=panel32.at[slot],
            send_sem=asend.at[d],
            recv_sem=arecv.at[d],
            device_id={"virt": peer},
            device_id_type=MESH,
        )

    def start_share(d, carry):
        share(d, v).start()
        return carry

    def wait_share(d, carry):
        share(d, lax.rem(v - d + nv, nv)).wait_recv()
        return carry

    def done_share(d, carry):
        share(d, v).wait_send()
        return carry

    lax.fori_loop(1, nv, start_share, 0)
    lax.fori_loop(1, nv, wait_share, 0)
    panel[...] = panel32[...].reshape(pairs, slab).astype(jnp.bfloat16)

    def message(side, c, t):
        peer = lax.rem(z + 1, n) if side == 0 else lax.rem(z + last, n)
        return pltpu.make_async_remote_copy(
            src_ref=sbuf.at[side, c, t - 1],
            dst_ref=rbuf.at[side, c, t - 1],
            send_sem=ssem.at[side, c, t - 1],
            recv_sem=rsem.at[side, c, t - 1],
            device_id={"opair": peer},
            device_id_type=MESH,
        )

    def part(c, owner):
        return acc[c, pl.ds(pl.multiple_of(owner * rows, rows), rows), :]

    def place(side):
        return z if side == 0 else last - z

    def owner_of(side, t):
        o = place(side) + n - t
        return o if side == 0 else last - o

    def compute(c):
        load(c).wait()
        slot = lax.rem(c, slots)
        acc[c] = jnp.zeros((pairs, width), jnp.float32)

        def step(k, carry):
            at = pl.multiple_of(k * step_rows, step_rows)
            block = ibuf[slot, pl.ds(at, step_rows)].reshape(step_rows, width)
            acc[c] += jnp.dot(
                panel[:, pl.ds(at, step_rows)], block, preferred_element_type=jnp.float32
            )
            return carry

        lax.fori_loop(0, slab // step_rows, step, 0)

        @pl.when(c + slots < chunks)
        def _():
            load(c + slots).start()

        for side in (0, 1):
            @pl.when(place(side) == 0)
            def _():
                for t in range(1, n):
                    encode(part(c, owner_of(side, t)), sbuf.at[side, c, t - 1], width)
                    message(side, c, t).start()

    def forward(c, t):
        for side in (0, 1):
            @pl.when((place(side) > 0) & (place(side) < t))
            def _():
                message(side, c, t - 1).wait_recv()
                total = part(c, owner_of(side, t)) + decode(rbuf.at[side, c, t - 2], width)
                encode(total, sbuf.at[side, c, t - 1], width)
                message(side, c, t).start()

    def finish(c):
        for side in (0, 1):
            @pl.when(place(side) > 0)
            def _():
                message(side, c, n - 1).wait_recv()
                at = pl.ds(pl.multiple_of(z * rows, rows), rows)
                acc[c, at, :] += decode(rbuf.at[side, c, n - 2], width)
        denominator = pe_ref[...] - ef_ref[c] - ep_ref[c]
        value = (part(c, z) + driver_ref[c].astype(jnp.float32)) / denominator
        out_ref[c] = jnp.where(in_ref[c] > 0, value, 0.0).astype(jnp.bfloat16)

    end_lag = n

    def turn(i, carry):
        @pl.when(i < chunks)
        def _():
            compute(i)

        for t in range(2, n):
            c = i - (t - 1)

            @pl.when((c >= 0) & (c < chunks))
            def _():
                forward(c, t)

        c = i - end_lag

        @pl.when(c >= 0)
        def _():
            finish(c)

        return carry

    lax.fori_loop(0, chunks + end_lag, turn, 0)
    lax.fori_loop(1, nv, done_share, 0)

    def done(c, carry):
        for side in (0, 1):
            for t in range(1, n):
                @pl.when((place(side) < t) & (place(side) < last))
                def _():
                    message(side, c, t).wait_send()
        return carry

    lax.fori_loop(0, chunks, done, 0)


def local(n, nv, amplitudes, integrals, driver, eps_occ, eps_vir, pair_occ, offsets, sizes):
    slab, a_count, bwidth = integrals.shape
    rows = driver.shape[0]
    pairs = rows * n
    ca = 16 if a_count % 16 == 0 else a_count
    chunks = a_count // ca
    width = ca * bwidth
    step_rows = 256 if slab % 256 == 0 else slab
    slots = min(4, chunks)

    hit = pair_occ[:, :, None] == jnp.arange(eps_occ.shape[0], dtype=jnp.int32)
    each = jnp.sum(jnp.where(hit, eps_occ, 0.0), axis=2)
    pair_energy = each[:, 0:1] + each[:, 1:2]
    e_pair = jnp.zeros((a_count, bwidth), jnp.float32)
    for k in range(eps_vir.shape[0] // bwidth):
        e_pair = jnp.where(
            (offsets == k * bwidth)[:, None], eps_vir[None, k * bwidth:(k + 1) * bwidth], e_pair
        )
    first = lax.axis_index("virt") * a_count
    e_first = lax.dynamic_slice_in_dim(eps_vir, first, a_count, 0)
    column = jnp.arange(bwidth, dtype=jnp.int32)
    inside = (column[None, :] < sizes[:, None]).astype(jnp.float32)
    e_first = jnp.broadcast_to(e_first[:, None], (a_count, bwidth))

    def flat(x):
        return x.reshape(chunks, 1, width)

    driver = driver.reshape(rows, chunks, width).transpose(1, 0, 2)
    vmem = pl.BlockSpec(memory_space=pltpu.VMEM)
    out = pl.pallas_call(
        functools.partial(kernel, n, nv, step_rows, slots),
        out_shape=jax.ShapeDtypeStruct((chunks, rows, width), jnp.bfloat16),
        in_specs=[vmem, pl.BlockSpec(memory_space=pl.ANY)] + [vmem] * 5,
        out_specs=vmem,
        scratch_shapes=[
            pltpu.VMEM((nv, pairs // nv, slab), jnp.float32),
            pltpu.VMEM((pairs, slab), jnp.bfloat16),
            pltpu.VMEM((slots, slab, ca, bwidth), jnp.bfloat16),
            pltpu.VMEM((chunks, pairs, width), jnp.float32),
            pltpu.VMEM((2, chunks, n - 1, rows, width + LANES), jnp.int16),
            pltpu.VMEM((2, chunks, n - 1, rows, width + LANES), jnp.int16),
            pltpu.SemaphoreType.DMA((slots,)),
            pltpu.SemaphoreType.DMA((nv,)),
            pltpu.SemaphoreType.DMA((nv,)),
            pltpu.SemaphoreType.DMA((2, chunks, n - 1)),
            pltpu.SemaphoreType.DMA((2, chunks, n - 1)),
        ],
        compiler_params=pltpu.CompilerParams(
            collective_id=0, has_side_effects=True, vmem_limit_bytes=56 * 1024 * 1024
        ),
        cost_estimate=pl.CostEstimate(
            flops=2 * pairs * slab * a_count * bwidth,
            bytes_accessed=2 * slab * a_count * bwidth,
            transcendentals=0,
        ),
    )(amplitudes, integrals, driver, pair_energy, flat(e_first), flat(e_pair), flat(inside))
    return out.transpose(1, 0, 2).reshape(rows, a_count, bwidth)


def solution(mesh):
    placed = (
        P("virt", "opair"),
        P("opair", "virt", None),
        P("opair", "virt", None),
        P(),
        P(),
        P("opair", None),
        P("virt"),
        P("virt"),
    )
    return jax.shard_map(
        functools.partial(local, mesh.shape["opair"], mesh.shape["virt"]),
        mesh=mesh, in_specs=placed, out_specs=P("opair", "virt", None), check_vma=False,
    )
```

time: 154 us -> 74.1 us (0.48)
  Pallas kernels: 0 us -> 60.5 us
  local copies, waits for them, and re-layouts: 68.1 us -> 9.22 us
  matrix products: 49.6 us -> 0 us
  between operations: 13.5 us -> 0.17 us
  blocking collectives: 10.9 us -> 0 us
  waiting for transfers between devices: 10.1 us -> 0 us
  other arithmetic: 1.55 us -> 3.91 us
    gather x3 -> x0, local copies, waits for them, and re-layouts: 66.6 us -> none  [the longest x1 65.3 us: local(): e_pair = jnp.take(eps_vir, b_index)]
    pallas_call x0 -> x1, Pallas kernels: none -> 60.5 us  [local(): pl.pallas_call(functools.partial(kernel, n, nv, step_rows, slots), out_sh...]
    dot_general x1 -> x0, matrix products: 49.6 us -> none  [local(): jnp.dot(panel, flat, preferred_element_type=jnp.float32)]
    all_gather x1 -> x0, blocking collectives: 10.9 us -> none  [local(): panel = lax.all_gather(amplitudes, 'virt', axis=0, tiled=True)]
    reduce_scatter x1 -> x0, waiting for transfers between devices: 10 us -> none  [local(): lax.psum_scatter(jnp.dot(panel, flat, preferred_element_type=jnp.float32)...]
    reshape x0 -> x3, local copies, waits for them, and re-layouts: none -> 3.39 us  [the longest x2 2.35 us: local(): driver = driver.reshape(rows, chunks, width).transpose(1, 0, 2)]
    broadcast_in_dim x0 -> x30, local copies, waits for them, and re-layouts: none -> 2.41 us  [the longest x28 1.62 us: local(): jnp.where((offsets == k * bwidth)[:, None], eps_vir[None, k * bwidth:(k +...]
  transfers between devices with their start and end apart: 1 -> 0, of which waited for: 1 -> 0; matrix products, arithmetic and copies ran while one was open for 44% -> 0% of each run, Pallas kernels for 0% -> 0%
where the time goes in v1:
time: 74.1 us; the launch traced here: 73.8 us
  Pallas kernels  60.5 us (82%)
  local copies, waits for them, and re-layouts  9.22 us (12%)
  other arithmetic  3.91 us (5%)
    pallas_call x1, Pallas kernels, local(): pl.pallas_call(functools.partial(kernel, n, nv, step_rows, slots), out_sh...  60.5 us
    reshape x2, local copies, waits for them, and re-layouts, local(): driver = driver.reshape(rows, chunks, width).transpose(1, 0, 2)  2.35 us
    broadcast_in_dim x28, local copies, waits for them, and re-layouts, local(): jnp.where((offsets == k * bwidth)[:, None], eps_vir[None, k * bwidth:(k +...  1.62 us

profile of v1, /device:TPU:0, one launch (start us, length us, event | category | flops | bytes accessed | tf_op | source)
XLA Modules:
  0.0 73.8 jit_solution(12244783354404060863)
XLA Ops:
  0.0 0.9 %select_reduce_fusion = f32[16,2]{0,1:T(2,128)S(1)} fusion(f32[200]{0:T(256)} %param.11, s32[16,2]{0,1:T(2,128)} %param.13), kind=kLoop, calls=%fused_computation.3 | loop fusion | flops 19168 | bytes 1056 | tf_op jit(solution)/shard_map/reduce_sum | solution.py:213
  0.9 0.7 lt.35
  1.6 0.7 broadcast_compare_fusion
  2.3 0.1 broadcast_in_dim.238
  2.3 0.1 broadcast_in_dim.226
  2.4 0.1 broadcast_in_dim.220
  2.5 0.1 broadcast_in_dim.214
  2.6 0.1 broadcast_in_dim.208
  2.7 0.1 broadcast_in_dim.202
  2.8 0.1 broadcast_in_dim.196
  2.9 0.1 broadcast_in_dim.232
  3.0 1.1 %fusion = (f32[128]{0:T(128)S(1)}, f32[128]{0:T(128)S(1)}, f32[128]{0:T(128)S(1)}, f32[128]{0:T(128)S(1)}, f32[128]{0:T(128)S(1)}, /*index=5*/f32[128]{0:T(128)S...) fusion(f32[1024]{0:T(1024)} %param.12, s32[]{:T(128)S(6)} %select_n.89), kind=kLoop, calls=%fused_computation.22 | loop fusion | bytes 9220 | tf_op jit(solution)/shard_map/slice | solution.py:218
  4.1 0.1 broadcast_in_dim.193
  4.2 0.1 copy.34
  4.2 0.1 copy.33
  4.3 0.6 add.6.pe_ref
  4.9 0.1 broadcast_in_dim.233
  5.0 0.1 broadcast_in_dim.197
  5.1 0.1 broadcast_in_dim.203
  5.2 0.1 broadcast_in_dim.209
  5.3 0.1 broadcast_in_dim.215
  5.4 0.1 broadcast_in_dim.221
  5.5 0.1 broadcast_in_dim.227
  5.5 0.1 broadcast_in_dim.239
  6.0 1.1 %select_select_fusion.ep_ref = f32[8,1,2048]{2,1,0:T(1,128)} fusion(pred[8,1,2048]{2,1,0:T(4,128)(4,1)S(1)} %broadcast_in_dim.245, pred[8,1,2048]{2,1,0:T(4,128)(4,1)S(1)} %broadcast_in_dim.246, pred[8,1,2048]{2,1,0:T(4,128)(4,1)S(1)} %broadcast_in_dim.247, pred[8,1,2048]{2,1,0:T(4,128)(4,1)S(1)} %broadcast_in_dim.248, ...), kind=kLoop, calls=%fused_computation.2 | loop fusion | flops 131072 | bytes 262144 | tf_op jit(solution)/shard_map/jit(_where)/select_n | solution.py:217
  7.1 0.7 broadcast_in_dim.194
  7.9 0.7 compare_convert_fusion.in_ref
  8.6 1.3 %reshape.390 = bf16[16,8,2048]{2,1,0:T(8,128)(2,1)S(1)} reshape(bf16[16,128,128]{2,1,0:T(8,128)(2,1)} %param.10) | data formatting | bytes 1048576 | tf_op jit(solution)/shard_map/reshape | solution.py:229
  9.8 1.1 %copy.36 = bf16[16,8,2048]{2,0,1:T(8,128)(2,1)} copy(bf16[16,8,2048]{2,1,0:T(8,128)(2,1)S(1)} %reshape.390) | data formatting | bytes 1048576 | tf_op jit(solution)/shard_map/reshape | solution.py:229
  10.9 60.5 %shard_map.82 = bf16[8,16,2048]{2,1,0:T(8,128)(2,1)} custom-call(bf16[8,1536]{1,0:T(8,128)(2,1)} %amp_ref.1, bf16[1536,128,128]{2,1,0:T(8,128)(2,1)} %int_ref.1, bf16[8,16,2048]{2,1,0:T(8,128)(2,1)} %bitcast.24, f32[16,1]{1,0:T(8,128)} %add.6.pe_ref, f32[8,1,2048]{2,1,0:T(1,128)} %bitcast.26, f32[8,1,2048]{2,1,0:T(1,128)} %select_select_fusion.ep_ref, ...), custom_call_target="tpu_custom_call" | custom-call | flops 3221225472 | bytes 50331648 | tf_op jit(solution)/shard_map/pallas_call | solution.py:231
  71.4 1.3 %copy.32 = bf16[16,8,2048]{2,1,0:T(8,128)(2,1)S(1)} copy(bf16[16,8,2048]{2,0,1:T(8,128)(2,1)} %bitcast.25) | data formatting | bytes 1048576 | tf_op jit(solution)/shard_map/transpose | solution.py:258
  72.8 1.0 %reshape.391 = bf16[16,128,128]{2,1,0:T(8,128)(2,1)} reshape(bf16[16,8,2048]{2,1,0:T(8,128)(2,1)S(1)} %copy.32) | data formatting | bytes 1048576 | tf_op jit(solution)/shard_map/reshape | solution.py:258
  (15 shorter events, 0.4 us)

commit v2 on v1

--- a/solution.py
+++ b/solution.py
@@ -10,6 +10,7 @@
 MESH = pl.DeviceIdType.MESH
 LANES = 128
 LEVELS = 32000.0
+OUTSIDE = 1e30
 
 
 def encode(x, out_ref, width):
@@ -28,8 +29,8 @@
 
 def kernel(
     n, nv, step_rows, slots,
-    amp_ref, int_ref, driver_ref, pe_ref, ef_ref, ep_ref, in_ref, out_ref,
-    panel32, panel, ibuf, acc, sbuf, rbuf,
+    amp_ref, int_ref, driver_ref, occ_ref, vir_ref, own_ref, pair_ref, off_ref, size_ref, out_ref,
+    panel32, panel, ibuf, acc, sbuf, rbuf, pe_ref, base_ref,
     isem, asend, arecv, ssem, rsem,
 ):
     z = lax.axis_index("opair")
@@ -39,14 +40,19 @@
     slab, ca = ibuf.shape[1], ibuf.shape[2]
     last = n - 1
 
-    def load(c):
+    bwidth = ibuf.shape[3]
+    blocks = slab // step_rows
+
+    def load(c, k):
         slot = lax.rem(c, slots)
+        at = pl.ds(pl.multiple_of(k * step_rows, step_rows), step_rows)
         return pltpu.make_async_copy(
-            int_ref.at[:, pl.ds(pl.multiple_of(c * ca, ca), ca), :], ibuf.at[slot], isem.at[slot]
+            int_ref.at[at, pl.ds(pl.multiple_of(c * ca, ca), ca), :], ibuf.at[slot, at], isem.at[slot, k]
         )
 
-    for c in range(min(slots, chunks)):
-        load(c).start()
+    for c in range(slots):
+        for k in range(blocks):
+            load(c, k).start()
 
     barrier = pltpu.get_barrier_semaphore()
 
@@ -66,6 +72,29 @@
         pl.semaphore_signal(barrier, inc=1, device_id={"opair": z + 1}, device_id_type=MESH)
 
     panel32[v] = amp_ref[...].astype(jnp.float32)
+
+    a_count = base_ref.shape[0]
+    occupied = lax.broadcasted_iota(jnp.int32, (rows, occ_ref.shape[1]), 1)
+    energy = jnp.zeros((rows, 1), jnp.float32)
+    for j in (0, 1):
+        hit = pair_ref[:, j:j + 1] == occupied
+        energy += jnp.sum(jnp.where(hit, occ_ref[...], 0.0), axis=1, keepdims=True)
+    pe_ref[...] = jnp.broadcast_to(energy, (rows, LANES))
+
+    across = lax.broadcasted_iota(jnp.int32, (a_count, a_count), 1)
+    same = lax.broadcasted_iota(jnp.int32, (a_count, a_count), 0) == across
+
+    def column(x):
+        return jnp.sum(jnp.where(same, x, 0.0), axis=1, keepdims=True)
+
+    e_first = column(own_ref[pl.ds(v, 1), :])
+    start = column(off_ref[...].astype(jnp.float32))
+    size = column(size_ref[...].astype(jnp.float32))
+    e_pair = jnp.zeros((a_count, bwidth), jnp.float32)
+    for k in range(vir_ref.shape[0]):
+        e_pair = jnp.where(start == float(k * bwidth), vir_ref[k:k + 1, :], e_pair)
+    t_index = lax.broadcasted_iota(jnp.int32, (a_count, bwidth), 1).astype(jnp.float32)
+    base_ref[...] = jnp.where(t_index < size, e_first + e_pair, OUTSIDE)
     beside = jnp.where(z > 0, 1, 0) + jnp.where(z < last, 1, 0)
     pl.semaphore_wait(barrier, nv - 1 + beside)
 
@@ -118,23 +147,24 @@
         return o if side == 0 else last - o
 
     def compute(c):
-        load(c).wait()
         slot = lax.rem(c, slots)
         acc[c] = jnp.zeros((pairs, width), jnp.float32)
 
         def step(k, carry):
+            load(c, k).wait()
             at = pl.multiple_of(k * step_rows, step_rows)
             block = ibuf[slot, pl.ds(at, step_rows)].reshape(step_rows, width)
             acc[c] += jnp.dot(
                 panel[:, pl.ds(at, step_rows)], block, preferred_element_type=jnp.float32
             )
+
+            @pl.when(c + slots < chunks)
+            def _():
+                load(c + slots, k).start()
+
             return carry
 
-        lax.fori_loop(0, slab // step_rows, step, 0)
-
-        @pl.when(c + slots < chunks)
-        def _():
-            load(c + slots).start()
+        lax.fori_loop(0, blocks, step, 0)
 
         for side in (0, 1):
             @pl.when(place(side) == 0)
@@ -159,9 +189,12 @@
                 message(side, c, n - 1).wait_recv()
                 at = pl.ds(pl.multiple_of(z * rows, rows), rows)
                 acc[c, at, :] += decode(rbuf.at[side, c, n - 2], width)
-        denominator = pe_ref[...] - ef_ref[c] - ep_ref[c]
-        value = (part(c, z) + driver_ref[c].astype(jnp.float32)) / denominator
-        out_ref[c] = jnp.where(in_ref[c] > 0, value, 0.0).astype(jnp.bfloat16)
+        held = pl.ds(pl.multiple_of(c * ca, ca), ca)
+        base = base_ref[held, :].reshape(1, width)
+        driver = driver_ref[:, held, :].astype(jnp.float32).reshape(rows, width)
+        value = (part(c, z) + driver) / (pe_ref[:, :1] - base)
+        value = jnp.where(base < OUTSIDE, value, 0.0)
+        out_ref[:, held, :] = value.reshape(rows, ca, bwidth).astype(jnp.bfloat16)
 
     end_lag = n
 
@@ -209,29 +242,11 @@
     step_rows = 256 if slab % 256 == 0 else slab
     slots = min(4, chunks)
 
-    hit = pair_occ[:, :, None] == jnp.arange(eps_occ.shape[0], dtype=jnp.int32)
-    each = jnp.sum(jnp.where(hit, eps_occ, 0.0), axis=2)
-    pair_energy = each[:, 0:1] + each[:, 1:2]
-    e_pair = jnp.zeros((a_count, bwidth), jnp.float32)
-    for k in range(eps_vir.shape[0] // bwidth):
-        e_pair = jnp.where(
-            (offsets == k * bwidth)[:, None], eps_vir[None, k * bwidth:(k + 1) * bwidth], e_pair
-        )
-    first = lax.axis_index("virt") * a_count
-    e_first = lax.dynamic_slice_in_dim(eps_vir, first, a_count, 0)
-    column = jnp.arange(bwidth, dtype=jnp.int32)
-    inside = (column[None, :] < sizes[:, None]).astype(jnp.float32)
-    e_first = jnp.broadcast_to(e_first[:, None], (a_count, bwidth))
-
-    def flat(x):
-        return x.reshape(chunks, 1, width)
-
-    driver = driver.reshape(rows, chunks, width).transpose(1, 0, 2)
     vmem = pl.BlockSpec(memory_space=pltpu.VMEM)
     out = pl.pallas_call(
         functools.partial(kernel, n, nv, step_rows, slots),
-        out_shape=jax.ShapeDtypeStruct((chunks, rows, width), jnp.bfloat16),
-        in_specs=[vmem, pl.BlockSpec(memory_space=pl.ANY)] + [vmem] * 5,
+        out_shape=jax.ShapeDtypeStruct(driver.shape, jnp.bfloat16),
+        in_specs=[vmem, pl.BlockSpec(memory_space=pl.ANY)] + [vmem] * 7,
         out_specs=vmem,
         scratch_shapes=[
             pltpu.VMEM((nv, pairs // nv, slab), jnp.float32),
@@ -240,7 +255,9 @@
             pltpu.VMEM((chunks, pairs, width), jnp.float32),
             pltpu.VMEM((2, chunks, n - 1, rows, width + LANES), jnp.int16),
             pltpu.VMEM((2, chunks, n - 1, rows, width + LANES), jnp.int16),
-            pltpu.SemaphoreType.DMA((slots,)),
+            pltpu.VMEM((rows, LANES), jnp.float32),
+            pltpu.VMEM((a_count, bwidth), jnp.float32),
+            pltpu.SemaphoreType.DMA((slots, slab // step_rows)),
             pltpu.SemaphoreType.DMA((nv,)),
             pltpu.SemaphoreType.DMA((nv,)),
             pltpu.SemaphoreType.DMA((2, chunks, n - 1)),
@@ -254,8 +271,11 @@
             bytes_accessed=2 * slab * a_count * bwidth,
             transcendentals=0,
         ),
-    )(amplitudes, integrals, driver, pair_energy, flat(e_first), flat(e_pair), flat(inside))
-    return out.transpose(1, 0, 2).reshape(rows, a_count, bwidth)
+    )(
+        amplitudes, integrals, driver, eps_occ.reshape(1, -1), eps_vir.reshape(-1, bwidth),
+        eps_vir.reshape(-1, a_count), pair_occ, offsets.reshape(1, -1), sizes.reshape(1, -1),
+    )
+    return out
 
 
 def solution(mesh):

time: 74.1 us -> 64.2 us (0.87)
  local copies, waits for them, and re-layouts: 9.22 us -> 3.24 us
  other arithmetic: 3.91 us -> 0 us
    reshape x3 -> x0, local copies, waits for them, and re-layouts: 3.39 us -> none  [the longest x2 2.35 us: local(): driver = driver.reshape(rows, chunks, width).transpose(1, 0, 2)]
    unnamed x2, local copies, waits for them, and re-layouts: 0.17 us -> 3.24 us
    broadcast_in_dim x30 -> x0, local copies, waits for them, and re-layouts: 2.41 us -> none  [the longest x28 1.62 us: local(): jnp.where((offsets == k * bwidth)[:, None], eps_vir[None, k * bwidth:(k +...]
    transpose x1 -> x0, local copies, waits for them, and re-layouts: 1.34 us -> none  [local(): return out.transpose(1, 0, 2).reshape(rows, a_count, bwidth)]
    slice x2 -> x0, local copies, waits for them, and re-layouts: 1.12 us -> none  [the longest x1 1.11 us: local(): eps_vir[None, k * bwidth:(k + 1) * bwidth]]
    select_n x1 -> x0, other arithmetic: 1.09 us -> none  [local(): jnp.where((offsets == k * bwidth)[:, None], eps_vir[None, k * bwidth:(k +...]
    reduce_sum x1 -> x0, other arithmetic: 0.85 us -> none  [local(): each = jnp.sum(jnp.where(hit, eps_occ, 0.0), axis=2)]
    lt x3 -> x0, local copies, waits for them, and re-layouts: 0.81 us -> none  [local(): inside = (column[None, :] < sizes[:, None]).astype(jnp.float32)]
where the time goes in v2:
time: 64.2 us; the launch traced here: 64 us
  Pallas kernels  60.8 us (95%)
  local copies, waits for them, and re-layouts  3.24 us (5%)
    pallas_call x1, Pallas kernels, local(): pl.pallas_call(functools.partial(kernel, n, nv, step_rows, slots), out_sh...  60.8 us
    unnamed x2, local copies, waits for them, and re-layouts  3.24 us

profile of v2, /device:TPU:0, one launch (start us, length us, event | category | flops | bytes accessed | tf_op | source)
XLA Modules:
  0.0 64.0 jit_solution(8220547447472943175)
XLA Ops:
  0.0 1.4 %copy.9.pair_ref = s32[16,2]{1,0:T(8,128)} copy(s32[16,2]{0,1:T(2,128)} %param.13) | data formatting | bytes 256 | tf_op args[5]
  1.4 60.8 %shard_map.82 = bf16[16,128,128]{2,1,0:T(8,128)(2,1)} custom-call(bf16[8,1536]{1,0:T(8,128)(2,1)} %amp_ref.1, bf16[1536,128,128]{2,1,0:T(8,128)(2,1)} %int_ref.1, bf16[16,128,128]{2,1,0:T(8,128)(2,1)} %driver_ref.1, f32[1,200]{1,0:T(1,128)} %bitcast.6, f32[8,128]{1,0:T(8,128)} %bitcast.4, f32[8,128]{1,0:T(8,128)} %bitcast.5, s32[16,2]{1,0:T(8,128)} %copy.9.pair_ref, ...), custom_call_target="tpu_custom_call" | custom-call | flops 3221225472 | bytes 50331648 | tf_op jit(solution)/shard_map/pallas_call | solution.py:246
  62.1 1.9 %copy.11 = bf16[16,128,128]{2,1,0:T(8,128)(2,1)} copy(bf16[16,128,128]{2,1,0:T(8,128)(2,1)} %shard_map.82) | data formatting | bytes 1048576

commit v3 on v2

--- a/solution.py
+++ b/solution.py
@@ -30,7 +30,7 @@
 def kernel(
     n, nv, step_rows, slots,
     amp_ref, int_ref, driver_ref, occ_ref, vir_ref, own_ref, pair_ref, off_ref, size_ref, out_ref,
-    panel32, panel, ibuf, acc, sbuf, rbuf, pe_ref, base_ref,
+    panel32, panel, ibuf, acc, sbuf, rbuf, pe_ref, base_ref, order, turned,
     isem, asend, arecv, ssem, rsem,
 ):
     z = lax.axis_index("opair")
@@ -71,6 +71,12 @@
     def _():
         pl.semaphore_signal(barrier, inc=1, device_id={"opair": z + 1}, device_id_type=MESH)
 
+    depth = order.shape[0]
+    group = depth // ca
+    to = lax.broadcasted_iota(jnp.int32, (depth, depth), 0)
+    source = lax.broadcasted_iota(jnp.int32, (depth, depth), 1)
+    wanted = lax.rem(to, group) * ca + to // group
+    order[...] = jnp.where(source == wanted, 1.0, 0.0).astype(jnp.bfloat16)
     panel32[v] = amp_ref[...].astype(jnp.float32)
 
     a_count = base_ref.shape[0]
@@ -153,7 +159,19 @@
         def step(k, carry):
             load(c, k).wait()
             at = pl.multiple_of(k * step_rows, step_rows)
-            block = ibuf[slot, pl.ds(at, step_rows)].reshape(step_rows, width)
+            for b in range(0, step_rows, 2 * group):
+                pair = [
+                    ibuf[slot, pl.ds(at + b + j * group, group)].reshape(group * ca, bwidth)
+                    for j in (0, 1)
+                ]
+                moved = jnp.dot(
+                    order[...], jnp.concatenate(pair, axis=1), preferred_element_type=jnp.float32
+                ).astype(jnp.bfloat16)
+                for j in (0, 1):
+                    turned[:, b + j * group:b + (j + 1) * group, :] = moved[
+                        :, j * bwidth:(j + 1) * bwidth
+                    ].reshape(ca, group, bwidth)
+            block = jnp.concatenate([turned[a] for a in range(ca)], axis=1)
             acc[c] += jnp.dot(
                 panel[:, pl.ds(at, step_rows)], block, preferred_element_type=jnp.float32
             )
@@ -239,7 +257,8 @@
     ca = 16 if a_count % 16 == 0 else a_count
     chunks = a_count // ca
     width = ca * bwidth
-    step_rows = 256 if slab % 256 == 0 else slab
+    step_rows = 512 if slab % 512 == 0 else slab
+    depth = 256
     slots = min(4, chunks)
 
     vmem = pl.BlockSpec(memory_space=pltpu.VMEM)
@@ -257,6 +276,8 @@
             pltpu.VMEM((2, chunks, n - 1, rows, width + LANES), jnp.int16),
             pltpu.VMEM((rows, LANES), jnp.float32),
             pltpu.VMEM((a_count, bwidth), jnp.float32),
+            pltpu.VMEM((depth, depth), jnp.bfloat16),
+            pltpu.VMEM((ca, step_rows, bwidth), jnp.bfloat16),
             pltpu.SemaphoreType.DMA((slots, slab // step_rows)),
             pltpu.SemaphoreType.DMA((nv,)),
             pltpu.SemaphoreType.DMA((nv,)),

time: 64.2 us -> 64.1 us (level)
  no operation moved by 1% of the time
where the time goes in v3:
time: 64.1 us; the launch traced here: 63.9 us
  Pallas kernels  60.7 us (95%)
  local copies, waits for them, and re-layouts  3.24 us (5%)
    pallas_call x1, Pallas kernels, local(): pl.pallas_call(functools.partial(kernel, n, nv, step_rows, slots), out_sh...  60.7 us
    unnamed x2, local copies, waits for them, and re-layouts  3.24 us

profile of v3, /device:TPU:0, one launch (start us, length us, event | category | flops | bytes accessed | tf_op | source)
XLA Modules:
  0.0 63.9 jit_solution(2486627365646940684)
XLA Ops:
  0.0 1.4 %copy.9.pair_ref = s32[16,2]{1,0:T(8,128)} copy(s32[16,2]{0,1:T(2,128)} %param.13) | data formatting | bytes 256 | tf_op args[5]
  1.4 60.7 %shard_map.82 = bf16[16,128,128]{2,1,0:T(8,128)(2,1)} custom-call(bf16[8,1536]{1,0:T(8,128)(2,1)} %amp_ref.1, bf16[1536,128,128]{2,1,0:T(8,128)(2,1)} %int_ref.1, bf16[16,128,128]{2,1,0:T(8,128)(2,1)} %driver_ref.1, f32[1,200]{1,0:T(1,128)} %bitcast.6, f32[8,128]{1,0:T(8,128)} %bitcast.4, f32[8,128]{1,0:T(8,128)} %bitcast.5, s32[16,2]{1,0:T(8,128)} %copy.9.pair_ref, ...), custom_call_target="tpu_custom_call" | custom-call | flops 3221225472 | bytes 50331648 | tf_op jit(solution)/shard_map/pallas_call | solution.py:265
  62.0 1.9 %copy.11 = bf16[16,128,128]{2,1,0:T(8,128)(2,1)} copy(bf16[16,128,128]{2,1,0:T(8,128)(2,1)} %shard_map.82) | data formatting | bytes 1048576

commit v4 on v2

--- a/solution.py
+++ b/solution.py
@@ -30,7 +30,7 @@
 def kernel(
     n, nv, step_rows, slots,
     amp_ref, int_ref, driver_ref, occ_ref, vir_ref, own_ref, pair_ref, off_ref, size_ref, out_ref,
-    panel32, panel, ibuf, acc, sbuf, rbuf, pe_ref, base_ref,
+    panel32, panel, ibuf, acc, sbuf, rbuf, pe_ref, base_ref, order, turned,
     isem, asend, arecv, ssem, rsem,
 ):
     z = lax.axis_index("opair")
@@ -72,29 +72,6 @@
         pl.semaphore_signal(barrier, inc=1, device_id={"opair": z + 1}, device_id_type=MESH)
 
     panel32[v] = amp_ref[...].astype(jnp.float32)
-
-    a_count = base_ref.shape[0]
-    occupied = lax.broadcasted_iota(jnp.int32, (rows, occ_ref.shape[1]), 1)
-    energy = jnp.zeros((rows, 1), jnp.float32)
-    for j in (0, 1):
-        hit = pair_ref[:, j:j + 1] == occupied
-        energy += jnp.sum(jnp.where(hit, occ_ref[...], 0.0), axis=1, keepdims=True)
-    pe_ref[...] = jnp.broadcast_to(energy, (rows, LANES))
-
-    across = lax.broadcasted_iota(jnp.int32, (a_count, a_count), 1)
-    same = lax.broadcasted_iota(jnp.int32, (a_count, a_count), 0) == across
-
-    def column(x):
-        return jnp.sum(jnp.where(same, x, 0.0), axis=1, keepdims=True)
-
-    e_first = column(own_ref[pl.ds(v, 1), :])
-    start = column(off_ref[...].astype(jnp.float32))
-    size = column(size_ref[...].astype(jnp.float32))
-    e_pair = jnp.zeros((a_count, bwidth), jnp.float32)
-    for k in range(vir_ref.shape[0]):
-        e_pair = jnp.where(start == float(k * bwidth), vir_ref[k:k + 1, :], e_pair)
-    t_index = lax.broadcasted_iota(jnp.int32, (a_count, bwidth), 1).astype(jnp.float32)
-    base_ref[...] = jnp.where(t_index < size, e_first + e_pair, OUTSIDE)
     beside = jnp.where(z > 0, 1, 0) + jnp.where(z < last, 1, 0)
     pl.semaphore_wait(barrier, nv - 1 + beside)
 
@@ -122,6 +99,63 @@
         return carry
 
     lax.fori_loop(1, nv, start_share, 0)
+
+    depth = order.shape[0]
+    group = depth // ca
+    to = lax.broadcasted_iota(jnp.int32, (depth, depth), 0)
+    source = lax.broadcasted_iota(jnp.int32, (depth, depth), 1)
+    wanted = lax.rem(to, group) * ca + to // group
+    order[...] = jnp.where(source == wanted, 1.0, 0.0).astype(jnp.bfloat16)
+
+    a_count = base_ref.shape[0]
+    def column(x):
+        size = x.shape[1]
+        across = lax.broadcasted_iota(jnp.int32, (size, size), 1)
+        same = lax.broadcasted_iota(jnp.int32, (size, size), 0) == across
+        return jnp.sum(jnp.where(same, x.astype(jnp.float32), 0.0), axis=1, keepdims=True)
+
+    occupied = lax.broadcasted_iota(jnp.int32, (rows, occ_ref.shape[1]), 1).astype(jnp.float32)
+    energy = jnp.zeros((rows, 1), jnp.float32)
+    for j in (0, 1):
+        hit = column(pair_ref[j:j + 1, :]) == occupied
+        energy += jnp.sum(jnp.where(hit, occ_ref[...], 0.0), axis=1, keepdims=True)
+    pe_ref[...] = jnp.broadcast_to(energy, (rows, LANES))
+
+    e_first = column(own_ref[pl.ds(v, 1), :])
+    start = column(off_ref[...])
+    size = column(size_ref[...])
+    e_pair = jnp.zeros((a_count, bwidth), jnp.float32)
+    for k in range(vir_ref.shape[0]):
+        e_pair = jnp.where(start == float(k * bwidth), vir_ref[k:k + 1, :], e_pair)
+    t_index = lax.broadcasted_iota(jnp.int32, (a_count, bwidth), 1).astype(jnp.float32)
+    base_ref[...] = jnp.where(t_index < size, e_first + e_pair, OUTSIDE)
+
+    def reorder(c, k):
+        load(c, k).wait()
+        slot = lax.rem(c, slots)
+        at = pl.multiple_of(k * step_rows, step_rows)
+        for b in range(0, step_rows, 2 * group):
+            pair = [
+                ibuf[slot, pl.ds(at + b + j * group, group)].reshape(group * ca, bwidth)
+                for j in (0, 1)
+            ]
+            moved = jnp.dot(
+                order[...], jnp.concatenate(pair, axis=1), preferred_element_type=jnp.float32
+            ).astype(jnp.bfloat16)
+            for j in (0, 1):
+                turned[k, :, b + j * group:b + (j + 1) * group, :] = moved[
+                    :, j * bwidth:(j + 1) * bwidth
+                ].reshape(ca, group, bwidth)
+
+        @pl.when(c + slots < chunks)
+        def _():
+            load(c + slots, k).start()
+
+    def reorder_first(k, carry):
+        reorder(0, k)
+        return carry
+
+    lax.fori_loop(0, blocks, reorder_first, 0)
     lax.fori_loop(1, nv, wait_share, 0)
     panel[...] = panel32[...].reshape(pairs, slab).astype(jnp.bfloat16)
 
@@ -147,21 +181,18 @@
         return o if side == 0 else last - o
 
     def compute(c):
-        slot = lax.rem(c, slots)
         acc[c] = jnp.zeros((pairs, width), jnp.float32)
 
         def step(k, carry):
-            load(c, k).wait()
+            @pl.when(c > 0)
+            def _():
+                reorder(c, k)
+
             at = pl.multiple_of(k * step_rows, step_rows)
-            block = ibuf[slot, pl.ds(at, step_rows)].reshape(step_rows, width)
+            block = jnp.concatenate([turned[k, a] for a in range(ca)], axis=1)
             acc[c] += jnp.dot(
                 panel[:, pl.ds(at, step_rows)], block, preferred_element_type=jnp.float32
             )
-
-            @pl.when(c + slots < chunks)
-            def _():
-                load(c + slots, k).start()
-
             return carry
 
         lax.fori_loop(0, blocks, step, 0)
@@ -194,7 +225,7 @@
         driver = driver_ref[:, held, :].astype(jnp.float32).reshape(rows, width)
         value = (part(c, z) + driver) / (pe_ref[:, :1] - base)
         value = jnp.where(base < OUTSIDE, value, 0.0)
-        out_ref[:, held, :] = value.reshape(rows, ca, bwidth).astype(jnp.bfloat16)
+        out_ref[:, held, :] = value.reshape(rows, ca, bwidth)
 
     end_lag = n
 
@@ -239,13 +270,14 @@
     ca = 16 if a_count % 16 == 0 else a_count
     chunks = a_count // ca
     width = ca * bwidth
-    step_rows = 256 if slab % 256 == 0 else slab
+    step_rows = 512 if slab % 512 == 0 else slab
+    depth = 256
     slots = min(4, chunks)
 
     vmem = pl.BlockSpec(memory_space=pltpu.VMEM)
     out = pl.pallas_call(
         functools.partial(kernel, n, nv, step_rows, slots),
-        out_shape=jax.ShapeDtypeStruct(driver.shape, jnp.bfloat16),
+        out_shape=jax.ShapeDtypeStruct(driver.shape, jnp.float32),
         in_specs=[vmem, pl.BlockSpec(memory_space=pl.ANY)] + [vmem] * 7,
         out_specs=vmem,
         scratch_shapes=[
@@ -257,6 +289,8 @@
             pltpu.VMEM((2, chunks, n - 1, rows, width + LANES), jnp.int16),
             pltpu.VMEM((rows, LANES), jnp.float32),
             pltpu.VMEM((a_count, bwidth), jnp.float32),
+            pltpu.VMEM((depth, depth), jnp.bfloat16),
+            pltpu.VMEM((slab // step_rows, ca, step_rows, bwidth), jnp.bfloat16),
             pltpu.SemaphoreType.DMA((slots, slab // step_rows)),
             pltpu.SemaphoreType.DMA((nv,)),
             pltpu.SemaphoreType.DMA((nv,)),
@@ -273,9 +307,9 @@
         ),
     )(
         amplitudes, integrals, driver, eps_occ.reshape(1, -1), eps_vir.reshape(-1, bwidth),
-        eps_vir.reshape(-1, a_count), pair_occ, offsets.reshape(1, -1), sizes.reshape(1, -1),
+        eps_vir.reshape(-1, a_count), pair_occ.T, offsets.reshape(1, -1), sizes.reshape(1, -1),
     )
-    return out
+    return out.astype(jnp.bfloat16)
 
 
 def solution(mesh):

time: 64.2 us -> 61.4 us (0.956)
  local copies, waits for them, and re-layouts: 3.24 us -> 0 us
  other arithmetic: 0 us -> 2.11 us
  Pallas kernels: 60.8 us -> 59.2 us
    unnamed x2 -> x0, local copies, waits for them, and re-layouts: 3.24 us -> none
    convert_element_type x0 -> x1, other arithmetic: none -> 2.11 us  [local(): return out.astype(jnp.bfloat16)]
    pallas_call x1, Pallas kernels: 60.8 us -> 59.2 us  [local(): pl.pallas_call(functools.partial(kernel, n, nv, step_rows, slots), out_sh...]
where the time goes in v4:
time: 61.4 us; the launch traced here: 61.3 us
  Pallas kernels  59.2 us (96%)
  other arithmetic  2.11 us (3%)
    pallas_call x1, Pallas kernels, local(): pl.pallas_call(functools.partial(kernel, n, nv, step_rows, slots), out_sh...  59.2 us
    convert_element_type x1, other arithmetic, local(): return out.astype(jnp.bfloat16)  2.11 us

profile of v4, /device:TPU:0, one launch (start us, length us, event | category | flops | bytes accessed | tf_op | source)
XLA Modules:
  0.0 61.3 jit_solution(81086696106213188)
XLA Ops:
  0.0 59.2 %shard_map.82 = f32[16,128,128]{2,1,0:T(8,128)} custom-call(bf16[8,1536]{1,0:T(8,128)(2,1)} %amp_ref.1, bf16[1536,128,128]{2,1,0:T(8,128)(2,1)} %int_ref.1, bf16[16,128,128]{2,1,0:T(8,128)(2,1)} %driver_ref.1, f32[1,200]{1,0:T(1,128)} %bitcast.7, f32[8,128]{1,0:T(8,128)} %bitcast.5, f32[8,128]{1,0:T(8,128)} %bitcast.6, s32[2,16]{1,0:T(2,128)} %bitcast.8, ...), custom_call_target="tpu_custom_call" | custom-call | flops 3221225472 | bytes 50331648 | tf_op jit(solution)/shard_map/pallas_call | solution.py:278
  59.2 2.1 %convert_element_type.3 = bf16[16,128,128]{2,1,0:T(8,128)(2,1)} convert(f32[16,128,128]{2,1,0:T(8,128)} %shard_map.82) | non-fusion elementwise | flops 262144 | bytes 1572864 | tf_op jit(solution)/shard_map/convert_element_type | solution.py:312

commit v5 on v4

--- a/solution.py
+++ b/solution.py
@@ -13,25 +13,30 @@
 OUTSIDE = 1e30
 
 
-def encode(x, out_ref, width):
+def diagonal(rows, lanes):
+    return lax.broadcasted_iota(jnp.int32, (rows, lanes), 0) == lax.broadcasted_iota(
+        jnp.int32, (rows, lanes), 1
+    )
+
+
+def encode(x, out_ref, top_ref):
     top = jnp.maximum(jnp.max(jnp.abs(x), axis=1, keepdims=True), 1e-30)
-    code = jnp.broadcast_to(jnp.ceil(jnp.log2(top) * 64.0), (x.shape[0], LANES))
-    gain = (jnp.exp2(code * (-1.0 / 64.0)) * LEVELS)[:, :1]
-    out_ref[:, :width] = jnp.round(x * gain).astype(jnp.int32).astype(jnp.int16)
-    out_ref[:, width:] = code.astype(jnp.int32).astype(jnp.int16)
-
-
-def decode(in_ref, width):
-    code = in_ref[:, width:].astype(jnp.int32).astype(jnp.float32)
-    gain = (jnp.exp2(code * (1.0 / 64.0)) * (1.0 / LEVELS))[:, :1]
-    return in_ref[:, :width].astype(jnp.int32).astype(jnp.float32) * gain
+    same = diagonal(x.shape[0], top_ref.shape[1])
+    top_ref[...] = jnp.sum(jnp.where(same, top, 0.0), axis=0, keepdims=True)
+    out_ref[...] = jnp.round(x * (LEVELS / top)).astype(jnp.int32).astype(jnp.int16)
+
+
+def decode(in_ref, top_ref):
+    same = diagonal(in_ref.shape[0], top_ref.shape[1])
+    top = jnp.sum(jnp.where(same, top_ref[...], 0.0), axis=1, keepdims=True)
+    return in_ref[...].astype(jnp.int32).astype(jnp.float32) * (top * (1.0 / LEVELS))
 
 
 def kernel(
     n, nv, step_rows, slots,
     amp_ref, int_ref, driver_ref, occ_ref, vir_ref, own_ref, pair_ref, off_ref, size_ref, out_ref,
-    panel32, panel, ibuf, acc, sbuf, rbuf, pe_ref, base_ref, order, turned,
-    isem, asend, arecv, ssem, rsem,
+    panel32, panel, ibuf, acc, sbuf, rbuf, stop, rtop, pe_ref, base_ref, order, turned,
+    isem, asend, arecv, ssem, rsem, stsem, rtsem,
 ):
     z = lax.axis_index("opair")
     v = lax.axis_index("virt")
@@ -159,16 +164,31 @@
     lax.fori_loop(1, nv, wait_share, 0)
     panel[...] = panel32[...].reshape(pairs, slab).astype(jnp.bfloat16)
 
-    def message(side, c, t):
+    def messages(side, c, t):
         peer = lax.rem(z + 1, n) if side == 0 else lax.rem(z + last, n)
-        return pltpu.make_async_remote_copy(
-            src_ref=sbuf.at[side, c, t - 1],
-            dst_ref=rbuf.at[side, c, t - 1],
-            send_sem=ssem.at[side, c, t - 1],
-            recv_sem=rsem.at[side, c, t - 1],
-            device_id={"opair": peer},
-            device_id_type=MESH,
-        )
+        return [
+            pltpu.make_async_remote_copy(
+                src_ref=source.at[side, c, t - 1],
+                dst_ref=target.at[side, c, t - 1],
+                send_sem=send.at[side, c, t - 1],
+                recv_sem=receive.at[side, c, t - 1],
+                device_id={"opair": peer},
+                device_id_type=MESH,
+            )
+            for source, target, send, receive in (
+                (stop, rtop, stsem, rtsem), (sbuf, rbuf, ssem, rsem),
+            )
+        ]
+
+    def send(side, c, t, total):
+        encode(total, sbuf.at[side, c, t - 1], stop.at[side, c, t - 1])
+        for copy in messages(side, c, t):
+            copy.start()
+
+    def receive(side, c, t):
+        for copy in messages(side, c, t):
+            copy.wait_recv()
+        return decode(rbuf.at[side, c, t - 1], rtop.at[side, c, t - 1])
 
     def part(c, owner):
         return acc[c, pl.ds(pl.multiple_of(owner * rows, rows), rows), :]
@@ -201,31 +221,27 @@
             @pl.when(place(side) == 0)
             def _():
                 for t in range(1, n):
-                    encode(part(c, owner_of(side, t)), sbuf.at[side, c, t - 1], width)
-                    message(side, c, t).start()
+                    send(side, c, t, part(c, owner_of(side, t)))
 
     def forward(c, t):
         for side in (0, 1):
             @pl.when((place(side) > 0) & (place(side) < t))
             def _():
-                message(side, c, t - 1).wait_recv()
-                total = part(c, owner_of(side, t)) + decode(rbuf.at[side, c, t - 2], width)
-                encode(total, sbuf.at[side, c, t - 1], width)
-                message(side, c, t).start()
+                send(side, c, t, part(c, owner_of(side, t)) + receive(side, c, t - 1))
 
     def finish(c):
         for side in (0, 1):
             @pl.when(place(side) > 0)
             def _():
-                message(side, c, n - 1).wait_recv()
+                arrived = receive(side, c, n - 1)
                 at = pl.ds(pl.multiple_of(z * rows, rows), rows)
-                acc[c, at, :] += decode(rbuf.at[side, c, n - 2], width)
+                acc[c, at, :] += arrived
         held = pl.ds(pl.multiple_of(c * ca, ca), ca)
         base = base_ref[held, :].reshape(1, width)
         driver = driver_ref[:, held, :].astype(jnp.float32).reshape(rows, width)
         value = (part(c, z) + driver) / (pe_ref[:, :1] - base)
         value = jnp.where(base < OUTSIDE, value, 0.0)
-        out_ref[:, held, :] = value.reshape(rows, ca, bwidth)
+        out_ref[:, held, :] = value.reshape(rows, ca, bwidth).astype(jnp.bfloat16)
 
     end_lag = n
 
@@ -257,7 +273,8 @@
             for t in range(1, n):
                 @pl.when((place(side) < t) & (place(side) < last))
                 def _():
-                    message(side, c, t).wait_send()
+                    for copy in messages(side, c, t):
+                        copy.wait_send()
         return carry
 
     lax.fori_loop(0, chunks, done, 0)
@@ -273,11 +290,12 @@
     step_rows = 512 if slab % 512 == 0 else slab
     depth = 256
     slots = min(4, chunks)
+    tops = -(-rows // LANES) * LANES
 
     vmem = pl.BlockSpec(memory_space=pltpu.VMEM)
     out = pl.pallas_call(
         functools.partial(kernel, n, nv, step_rows, slots),
-        out_shape=jax.ShapeDtypeStruct(driver.shape, jnp.float32),
+        out_shape=jax.ShapeDtypeStruct(driver.shape, jnp.bfloat16),
         in_specs=[vmem, pl.BlockSpec(memory_space=pl.ANY)] + [vmem] * 7,
         out_specs=vmem,
         scratch_shapes=[
@@ -285,8 +303,10 @@
             pltpu.VMEM((pairs, slab), jnp.bfloat16),
             pltpu.VMEM((slots, slab, ca, bwidth), jnp.bfloat16),
             pltpu.VMEM((chunks, pairs, width), jnp.float32),
-            pltpu.VMEM((2, chunks, n - 1, rows, width + LANES), jnp.int16),
-            pltpu.VMEM((2, chunks, n - 1, rows, width + LANES), jnp.int16),
+            pltpu.VMEM((2, chunks, n - 1, rows, width), jnp.int16),
+            pltpu.VMEM((2, chunks, n - 1, rows, width), jnp.int16),
+            pltpu.VMEM((2, chunks, n - 1, 1, tops), jnp.float32),
+            pltpu.VMEM((2, chunks, n - 1, 1, tops), jnp.float32),
             pltpu.VMEM((rows, LANES), jnp.float32),
             pltpu.VMEM((a_count, bwidth), jnp.float32),
             pltpu.VMEM((depth, depth), jnp.bfloat16),
@@ -294,6 +314,8 @@
             pltpu.SemaphoreType.DMA((slots, slab // step_rows)),
             pltpu.SemaphoreType.DMA((nv,)),
             pltpu.SemaphoreType.DMA((nv,)),
+            pltpu.SemaphoreType.DMA((2, chunks, n - 1)),
+            pltpu.SemaphoreType.DMA((2, chunks, n - 1)),
             pltpu.SemaphoreType.DMA((2, chunks, n - 1)),
             pltpu.SemaphoreType.DMA((2, chunks, n - 1)),
         ],
@@ -309,7 +331,7 @@
         amplitudes, integrals, driver, eps_occ.reshape(1, -1), eps_vir.reshape(-1, bwidth),
         eps_vir.reshape(-1, a_count), pair_occ.T, offsets.reshape(1, -1), sizes.reshape(1, -1),
     )
-    return out.astype(jnp.bfloat16)
+    return out
 
 
 def solution(mesh):

time: 61.4 us -> 59.8 us (0.974)
  other arithmetic: 2.11 us -> 0 us
  local copies, waits for them, and re-layouts: 0 us -> 1.89 us
  Pallas kernels: 59.2 us -> 57.8 us
    convert_element_type x1 -> x0, other arithmetic: 2.11 us -> none  [local(): return out.astype(jnp.bfloat16)]
    unnamed x0 -> x1, local copies, waits for them, and re-layouts: none -> 1.89 us
    pallas_call x1, Pallas kernels: 59.2 us -> 57.8 us  [local(): pl.pallas_call(functools.partial(kernel, n, nv, step_rows, slots), out_sh...]
where the time goes in v5:
time: 59.8 us; the launch traced here: 59.7 us
  Pallas kernels  57.8 us (97%)
  local copies, waits for them, and re-layouts  1.89 us (3%)
    pallas_call x1, Pallas kernels, local(): pl.pallas_call(functools.partial(kernel, n, nv, step_rows, slots), out_sh...  57.8 us
    unnamed x1, local copies, waits for them, and re-layouts  1.89 us

profile of v5, /device:TPU:0, one launch (start us, length us, event | category | flops | bytes accessed | tf_op | source)
XLA Modules:
  0.0 59.7 jit_solution(1255597066685807237)
XLA Ops:
  0.0 57.8 %shard_map.82 = bf16[16,128,128]{2,1,0:T(8,128)(2,1)} custom-call(bf16[8,1536]{1,0:T(8,128)(2,1)} %amp_ref.1, bf16[1536,128,128]{2,1,0:T(8,128)(2,1)} %int_ref.1, bf16[16,128,128]{2,1,0:T(8,128)(2,1)} %driver_ref.1, f32[1,200]{1,0:T(1,128)} %bitcast.7, f32[8,128]{1,0:T(8,128)} %bitcast.5, f32[8,128]{1,0:T(8,128)} %bitcast.6, s32[2,16]{1,0:T(2,128)} %bitcast.8, ...), custom_call_target="tpu_custom_call" | custom-call | flops 3221225472 | bytes 50331648 | tf_op jit(solution)/shard_map/pallas_call | solution.py:296
  57.8 1.9 %copy.10 = bf16[16,128,128]{2,1,0:T(8,128)(2,1)} copy(bf16[16,128,128]{2,1,0:T(8,128)(2,1)} %shard_map.82) | data formatting | bytes 1048576
